TPU v7x, 32 devices: a whole 2x2x4 slice. The times are simulated.
32 devices in a mesh: row: 8 (over z, x), rep: 4 (over y, core).
Axes of the slice: x: 2, y: 2, z: 4, core: 2. Of those that a mesh axis runs over, the one named last changes fastest.
Arguments:
- features: bfloat16 [8192, 256], P('row'), may hold values from -6 to 6
- block_cols: int32 [64, 4, 12], P('row', 'rep'), may hold values from 0 to 63, as said below
- block_vals: bfloat16 [64, 4, 12, 128, 128], P('row', 'rep'), may hold values from -0.078125 to 0.078125
- weight: bfloat16 [256, 256], replicated, may hold values from -0.375 to 0.375
- cotangent: bfloat16 [8192, 256], P(('row', 'rep')), may hold values from -6 to 6
Outputs:
- output_rows: bfloat16 [8192, 256], P(('row', 'rep'))
- grad_weight: float32 [256, 256], replicated
- grad_features: float32 [8192, 256], P(('row', 'rep'))
Inputs may be any that keep to these rules, and one draw needn't show every extreme that they name: For a node block b of row group g = b // 8 and quarter index r, every entry block_cols[b, r, s] equals h * 8 + r * 2 + q with h a row group within 3 of g (and inside the grid) and 0 <= q < 2; entries may repeat.
All inputs are finite; a program needn't handle non-finite values.
Results may differ from a plain program's by a relative error of at most 0.0065.
Values may be sent and summed in bfloat16 or wider, within the bound.
A program may use at most 64 MiB of HBM per device.

v0:
```python
import functools

import jax
import jax.numpy as jnp
from jax import lax
from jax.experimental import pallas as pl
from jax.experimental.pallas import tpu as pltpu
from jax.sharding import PartitionSpec as P

HALF = 3
SECTIONS = 2 * HALF + 1


def flip(index, bit):
    return index + bit * (1 - 2 * ((index // bit) % 2))


def flip_all(index, mask):
    bit = 1
    while bit <= mask:
        if mask & bit:
            index = flip(index, bit)
        bit *= 2
    return index


def remote(src, dst, send_sem, recv_sem, device):
    return pltpu.make_async_remote_copy(
        src_ref=src,
        dst_ref=dst,
        send_sem=send_sem,
        recv_sem=recv_sem,
        device_id=device,
        device_id_type=pl.DeviceIdType.MESH,
    )


def layer_kernel(
    sizes,
    plan_ref, features_ref, vals_ref, weight_ref, cotangent_ref,
    out_ref, grad_weight_ref, grad_features_ref,
    vals, turned, weight_own, cotangent, window, part_send, part_recv, near, far, run,
    back_send, back_recv, gw_send, gw_recv, gw_half, gw_across, bf_send, bf_recv, gw_all,
    local_sem, a_send, a_recv, b_send, b_recv, c_send, c_recv,
    d_send, d_recv, e_send, e_recv, f_send, f_recv, g_send, g_recv,
):
    rows, reps, quart, slots, blk, blocks = sizes
    pairs = blocks * slots
    spots = SECTIONS * quart
    padded = pairs + 2 * spots
    steps = padded // 2
    row = lax.axis_index("row")
    rep = lax.axis_index("rep")
    bits = [1 << k for k in range(rows.bit_length() - 1)]
    offsets = [d for d in (3, -3, 2, -2, 1, -1)]
    masks = sorted(range(1, reps), key=lambda m: -m)

    def inside(d):
        return jnp.logical_and(row + d >= 0, row + d < rows)

    vals_copy = pltpu.make_async_copy(vals_ref, vals, local_sem.at[0])
    vals_copy.start()
    weight_copy = pltpu.make_async_copy(weight_ref, weight_own, local_sem.at[2])
    weight_copy.start()
    cotangent_copy = pltpu.make_async_copy(cotangent_ref, cotangent, local_sem.at[3])
    cotangent_copy.start()
    own = features_ref.at[pl.ds(rep * quart, quart)]
    own_copy = pltpu.make_async_copy(own, window.at[pl.ds(HALF * quart, quart)], local_sem.at[1])
    own_copy.start()

    barrier = pltpu.get_barrier_semaphore()
    expected = reps - 1
    for d in offsets:
        @pl.when(inside(d))
        def _():
            pl.semaphore_signal(
                barrier, inc=1, device_id=(row + d, rep), device_id_type=pl.DeviceIdType.MESH
            )
        expected = expected + inside(d).astype(jnp.int32)
    for bit in bits:
        if bit > 2:
            pl.semaphore_signal(
                barrier, inc=1, device_id=(flip(row, bit), rep),
                device_id_type=pl.DeviceIdType.MESH,
            )
            expected = expected + 1
    for mask in masks:
        pl.semaphore_signal(
            barrier, inc=1, device_id=(row, flip_all(rep, mask)),
            device_id_type=pl.DeviceIdType.MESH,
        )
    pl.semaphore_wait(barrier, expected)

    def section(ref, j):
        return ref.at[pl.ds(j * quart, quart)]

    def feature_copy(d):
        return remote(
            own, section(window, HALF - d), a_send.at[HALF - d], a_recv.at[HALF - d],
            (row + d, rep),
        )

    for d in offsets:
        @pl.when(inside(d))
        def _():
            feature_copy(d).start()

        @pl.when(jnp.logical_not(inside(d)))
        def _():
            for q in range(quart):
                window[(HALF + d) * quart + q] = jnp.zeros(window.shape[1:], window.dtype)
                back_recv[(HALF + d) * quart + q] = jnp.zeros(
                    back_recv.shape[1:], back_recv.dtype
                )
    vals_copy.wait()

    turned[pairs] = jnp.zeros((blk, blk), turned.dtype)

    def turn(p, carry):
        turned[p] = vals[p].T
        return carry

    lax.fori_loop(0, pairs, turn, 0, unroll=8)
    own_copy.wait()
    weight_copy.wait()
    cotangent_copy.wait()
    for d in offsets:
        @pl.when(inside(d))
        def _():
            remote(
                own, section(window, HALF + d), a_send.at[HALF + d], a_recv.at[HALF + d],
                (row + d, rep),
            ).wait_recv()

    def partial(b):
        total = None
        for s in range(0, slots, 2):
            left = jnp.concatenate([vals[b * slots + s], vals[b * slots + s + 1]], axis=1)
            right = jnp.concatenate(
                [window[plan_ref[b * slots + s]], window[plan_ref[b * slots + s + 1]]], axis=0
            )
            term = jnp.dot(left, right, preferred_element_type=jnp.float32)
            total = term if total is None else total + term
        return total

    across, beside, opposite = flip(rep, 2), flip(rep, 1), flip_all(rep, 3)

    def partial_quarter(target):
        return jnp.concatenate([partial(target * quart + q) for q in range(quart)], axis=0)

    def part_copy(stage):
        return remote(
            part_send.at[stage], part_recv.at[stage], b_send.at[stage], b_recv.at[stage],
            (row, across if stage == 1 else beside),
        )

    part_send[0] = partial_quarter(opposite).astype(jnp.bfloat16)
    part_copy(0).start()
    total = partial_quarter(across)
    part_copy(0).wait_recv()
    part_send[1] = (total + part_recv[0].astype(jnp.float32)).astype(jnp.bfloat16)
    part_copy(1).start()
    part_send[2] = partial_quarter(beside).astype(jnp.bfloat16)
    part_copy(2).start()
    total = partial_quarter(rep)
    part_copy(2).wait_recv()
    total = total + part_recv[2].astype(jnp.float32)
    part_copy(1).wait_recv()
    total = total + part_recv[1].astype(jnp.float32)

    aggregate = total.astype(jnp.bfloat16)
    weight = weight_own[...]
    preact = jnp.dot(aggregate, weight, preferred_element_type=jnp.float32)
    sigmoid_pre = jax.nn.sigmoid(preact)
    grad_pre = (
        cotangent[...].astype(jnp.float32)
        * sigmoid_pre
        * (1.0 + preact * (1.0 - sigmoid_pre))
    ).astype(jnp.bfloat16)
    back_own = lax.dot_general(
        grad_pre, weight, (((1,), (1,)), ((), ())), preferred_element_type=jnp.float32
    ).astype(jnp.bfloat16)
    core, chip = rep % 2, rep // 2
    for q in range(quart):
        near[core * quart + q] = back_own[q * blk:(q + 1) * blk]

    def back_copy(stage):
        src, dst, target = ((near, far, across), (near, near, beside), (far, far, beside))[stage]
        return remote(
            section(src, core), section(dst, core), c_send.at[stage], c_recv.at[stage],
            (row, target),
        )

    back_copy(0).start()
    back_copy(1).start()
    out_ref[...] = (preact * sigmoid_pre).astype(jnp.bfloat16)

    gw_send[...] = lax.dot_general(
        aggregate, grad_pre, (((0,), (0,)), ((), ())), preferred_element_type=jnp.float32
    )
    half_rows = gw_send.shape[0] // 2
    share = half_rows // 2

    def share_of(ref, owner):
        return ref.at[pl.ds(((owner % 2) * 2 + owner // 2) * share, share)]

    def beside_copy():
        return remote(
            gw_send.at[pl.ds((1 - core) * half_rows, half_rows)], gw_recv,
            e_send.at[0], e_recv.at[0], (row, beside),
        )

    def across_copy():
        return remote(
            gw_half.at[pl.ds((1 - chip) * share, share)], gw_across,
            e_send.at[1], e_recv.at[1], (row, across),
        )

    def row_copy(k):
        return remote(
            bf_send.at[k], bf_recv.at[k], f_send.at[k], f_recv.at[k], (flip(row, bits[k]), rep)
        )

    def gather_copy(mask, owner):
        spot = share_of(gw_all, owner)
        return remote(
            spot, spot, g_send.at[mask - 1], g_recv.at[mask - 1], (row, flip_all(rep, mask))
        )

    beside_copy().start()
    beside_copy().wait_recv()
    gw_half[...] = gw_send[pl.ds(core * half_rows, half_rows)] + gw_recv[...]
    across_copy().start()
    back_copy(1).wait_recv()

    def backward(source, start, stop, acc):
        def step(k, acc):
            left = jnp.concatenate(
                [turned[plan_ref[pairs + 2 * k]], turned[plan_ref[pairs + 2 * k + 1]]], axis=1
            )
            right = jnp.concatenate(
                [
                    source[plan_ref[pairs + padded + 2 * k]],
                    source[plan_ref[pairs + padded + 2 * k + 1]],
                ],
                axis=0,
            )
            keep = plan_ref[pairs + 2 * padded + k]
            term = jnp.dot(left, right, preferred_element_type=jnp.float32)
            acc = jnp.where(keep > 0, acc, 0.0) + term
            run[k] = acc
            return acc

        return lax.fori_loop(start, stop, step, acc, unroll=5)

    zeros = jnp.zeros(run.shape[1:], jnp.float32)
    half = steps // 2
    fifth = half // 10 * 5
    acc = backward(near, 0, fifth, zeros)
    back_copy(0).wait_recv()
    back_copy(2).start()
    across_copy().wait_recv()
    bf_send[0] = gw_half[pl.ds(chip * share, share)] + gw_across[...]
    row_copy(0).start()
    backward(near, fifth, half, acc)
    back_copy(2).wait_recv()
    row_copy(0).wait_recv()
    bf_send[1] = bf_send[0] + bf_recv[0]
    row_copy(1).start()
    acc = backward(far, half, half + fifth, zeros)
    row_copy(1).wait_recv()
    bf_send[2] = bf_send[1] + bf_recv[1]
    row_copy(2).start()
    backward(far, half + fifth, steps, acc)

    def section_sum(j, q):
        found = []
        for c in (j * quart + q, spots + j * quart + q):
            last = plan_ref[pairs + 2 * padded + steps + c]
            some = plan_ref[pairs + 2 * padded + steps + 2 * spots + c]
            found.append(jnp.where(some > 0, run[last], 0.0))
        return found[0] + found[1]

    def grad_copy(d):
        return remote(
            section(back_send, HALF + d), section(back_recv, HALF - d), d_send.at[HALF - d],
            d_recv.at[HALF - d], (row + d, rep),
        )

    for d in offsets:
        for q in range(quart):
            back_send[(HALF + d) * quart + q] = section_sum(HALF + d, q).astype(jnp.bfloat16)

        @pl.when(inside(d))
        def _():
            grad_copy(d).start()

    for k in range(2, len(bits)):
        row_copy(k).wait_recv()
        summed = bf_send[k] + bf_recv[k]
        if k + 1 < len(bits):
            bf_send[k + 1] = summed
            row_copy(k + 1).start()
    gw_all[pl.ds((core * 2 + chip) * share, share)] = summed
    for mask in masks:
        gather_copy(mask, rep).start()

    for d in reversed(offsets):
        @pl.when(inside(d))
        def _():
            remote(
                section(back_send, HALF + d), section(back_recv, HALF + d), d_send.at[HALF + d],
                d_recv.at[HALF + d], (row + d, rep),
            ).wait_recv()
    for q in range(quart):
        result = section_sum(HALF, q)
        for d in offsets:
            result = result + back_recv[(HALF + d) * quart + q].astype(jnp.float32)
        grad_features_ref[q * blk:(q + 1) * blk] = result

    for mask in reversed(masks):
        gather_copy(mask, flip_all(rep, mask)).wait_recv()
    grad_weight_ref[...] = gw_all[...] * (rows * blocks * blk) ** (-0.5)

    for d in offsets:
        @pl.when(inside(d))
        def _():
            feature_copy(d).wait_send()
            grad_copy(d).wait_send()
    for mask in masks:
        part_copy(mask - 1).wait_send()
        back_copy(mask - 1).wait_send()
        gather_copy(mask, rep).wait_send()
    beside_copy().wait_send()
    across_copy().wait_send()
    for k in range(len(bits)):
        row_copy(k).wait_send()


def store_kernel(a_ref, b_ref, c_ref, a_out, b_out, c_out, sems):
    copies = [
        pltpu.make_async_copy(src, dst, sems.at[k])
        for k, (src, dst) in enumerate(((a_ref, a_out), (b_ref, b_out), (c_ref, c_out)))
    ]
    for copy in copies:
        copy.start()
    for copy in copies:
        copy.wait()


def make_plan(block_cols, quart):
    blocks, slots = block_cols.shape
    pairs = blocks * slots
    spots = SECTIONS * quart
    first = (lax.axis_index("row") - HALF) * blocks + lax.axis_index("rep") * quart
    moved = block_cols.reshape(pairs) - first
    slot = (moved // blocks) * quart + moved % blocks
    order = jnp.arange(pairs, dtype=jnp.int32)
    far = (order // slots // quart) // 2 != lax.axis_index("rep") // 2
    bin_of = slot + jnp.where(far, spots, 0)
    spot = jnp.arange(2 * spots, dtype=jnp.int32)
    half = (pairs // 2 + spots) // 2
    count = jnp.sum((bin_of[:, None] == spot[None, :]).astype(jnp.int32), axis=0)
    width = (count + 1) // 2
    same_half = (spot[:, None] // spots) == (spot[None, :] // spots)
    before = same_half & (spot[:, None] < spot[None, :])
    start = jnp.sum(jnp.where(before, width[:, None], 0), axis=0) + half * (spot // spots)
    rank = jnp.sum(
        ((bin_of[:, None] == bin_of[None, :]) & (order[:, None] < order[None, :])).astype(
            jnp.int32
        ),
        axis=0,
    )
    base = jnp.sum(jnp.where(spot[None, :] == bin_of[:, None], start[None, :], 0), axis=1)
    place = 2 * base + rank
    hot = place[:, None] == jnp.arange(4 * half, dtype=jnp.int32)[None, :]
    pair = pairs + jnp.sum(jnp.where(hot, order[:, None] - pairs, 0), axis=0)
    block = jnp.sum(jnp.where(hot, order[:, None] // slots % (2 * quart), 0), axis=0)
    step = jnp.arange(2 * half, dtype=jnp.int32)
    first_of = (start[:, None] == step[None, :]) & (count[:, None] > 0)
    keep = 1 - jnp.sum(first_of.astype(jnp.int32), axis=0)
    last = jnp.maximum(start + width - 1, 0)
    return jnp.concatenate([slot, pair, block, keep, last, count])


def on_device(rows, reps, features, block_cols, block_vals, weight, cotangent):
    group_rows, hidden = features.shape
    blocks, _, slots = block_cols.shape
    blk = block_vals.shape[-1]
    quart = blocks // reps
    pairs = blocks * slots
    own_rows = quart * blk
    levels = rows.bit_length() - 1
    share = hidden // reps
    plan = make_plan(block_cols[:, 0, :], quart)
    dma = pltpu.SemaphoreType.DMA
    bf16, f32 = jnp.bfloat16, jnp.float32
    vmem = pl.BlockSpec(memory_space=pltpu.VMEM)
    hbm = pl.BlockSpec(memory_space=pl.ANY)
    results = pl.pallas_call(
        functools.partial(layer_kernel, (rows, reps, quart, slots, blk, blocks)),
        out_shape=(
            jax.ShapeDtypeStruct((own_rows, hidden), bf16),
            jax.ShapeDtypeStruct((hidden, hidden), f32),
            jax.ShapeDtypeStruct((own_rows, hidden), f32),
        ),
        in_specs=[pl.BlockSpec(memory_space=pltpu.SMEM), hbm, hbm, hbm, hbm],
        out_specs=(vmem, vmem, vmem),
        scratch_shapes=[
            pltpu.VMEM((pairs, blk, blk), bf16),
            pltpu.VMEM((pairs + 1, blk, blk), bf16),
            pltpu.VMEM((hidden, hidden), bf16),
            pltpu.VMEM((own_rows, hidden), bf16),
            pltpu.VMEM((SECTIONS * quart, blk, hidden), bf16),
            pltpu.VMEM((reps - 1, own_rows, hidden), bf16),
            pltpu.VMEM((reps - 1, own_rows, hidden), bf16),
            pltpu.VMEM((blocks // 2, blk, hidden), bf16),
            pltpu.VMEM((blocks // 2, blk, hidden), bf16),
            pltpu.VMEM((pairs // 2 + SECTIONS * quart, blk, hidden), f32),
            pltpu.VMEM((SECTIONS * quart, blk, hidden), bf16),
            pltpu.VMEM((SECTIONS * quart, blk, hidden), bf16),
            pltpu.VMEM((hidden, hidden), f32),
            pltpu.VMEM((2 * share, hidden), f32),
            pltpu.VMEM((2 * share, hidden), f32),
            pltpu.VMEM((share, hidden), f32),
            pltpu.VMEM((levels, share, hidden), f32),
            pltpu.VMEM((levels, share, hidden), f32),
            pltpu.VMEM((hidden, hidden), f32),
            dma((4,)),
            dma((SECTIONS,)), dma((SECTIONS,)),
            dma((reps - 1,)), dma((reps - 1,)),
            dma((reps - 1,)), dma((reps - 1,)),
            dma((SECTIONS,)), dma((SECTIONS,)),
            dma((reps - 1,)), dma((reps - 1,)),
            dma((levels,)), dma((levels,)),
            dma((reps - 1,)), dma((reps - 1,)),
        ],
        compiler_params=pltpu.CompilerParams(
            collective_id=0, has_side_effects=True, vmem_limit_bytes=60 * 1024 * 1024
        ),
        cost_estimate=pl.CostEstimate(
            flops=4 * pairs * blk * blk * hidden, bytes_accessed=pairs * blk * blk * 2,
            transcendentals=own_rows * hidden,
        ),
    )(
        plan,
        features.reshape(blocks, blk, hidden),
        block_vals.reshape(pairs, blk, blk),
        weight,
        cotangent,
    )
    return pl.pallas_call(
        store_kernel,
        out_shape=tuple(jax.ShapeDtypeStruct(r.shape, r.dtype) for r in results),
        in_specs=[hbm, hbm, hbm],
        out_specs=(hbm, hbm, hbm),
        scratch_shapes=[dma((3,))],
        compiler_params=pltpu.CompilerParams(vmem_limit_bytes=60 * 1024 * 1024),
        cost_estimate=pl.CostEstimate(
            flops=0, bytes_accessed=20 * own_rows * hidden, transcendentals=0
        ),
    )(*results)


def solution(mesh):
    return jax.shard_map(
        functools.partial(on_device, mesh.shape["row"], mesh.shape["rep"]),
        mesh=mesh,
        in_specs=(
            P("row", None),
            P("row", "rep", None),
            P("row", "rep", None, None, None),
            P(),
            P(("row", "rep"), None),
        ),
        out_specs=(P(("row", "rep"), None), P(), P(("row", "rep"), None)),
        check_vma=False,
    )
```

profile of v0, /device:TPU:10, one launch (start us, length us, event | category | flops | bytes accessed | tf_op | source)
XLA Modules:
  0.0 72.9 jit_solution(15626776742862129467)
XLA Ops:
  0.7 0.7 subtract_reduce_fusion
  1.4 0.1 sub.77
  1.5 0.1 convert_reduce_fusion.2
  1.6 0.1 convert_reduce_fusion
  1.7 0.1 select_reduce_fusion.3
  1.8 0.1 convert_reduce_fusion.1
  1.9 0.1 select_reduce_fusion.2
  2.0 0.1 select_reduce_fusion
  2.2 0.7 concatenate.3.plan_ref
  2.8 49.0 %shard_map.76 = (bf16[256,256]{1,0:T(8,128)(2,1)}, f32[256,256]{1,0:T(8,128)}, f32[256,256]{1,0:T(8,128)}) custom-call(s32[462]{0:T(512)} %concatenate.3.plan_ref, bf16[8,128,256]{2,1,0:T(8,128)(2,1)} %bitcast.3, bf16[96,128,128]{2,1,0:T(8,128)(2,1)} %bitcast.2, bf16[256,256]{1,0:T(8,128)(2,1)} %weight_ref.1, bf16[256,256]{1,0:T(8,128)(2,1)} %cotangent_ref.1), custom_call_target="tpu_custom_call" | custom-call | flops 1610612736 | bytes 3145728 | tf_op jit(solution)/shard_map/pallas_call | solution.py:400
  51.9 21.0 %shard_map.77 = (bf16[256,256]{1,0:T(8,128)(2,1)}, f32[256,256]{1,0:T(8,128)}, f32[256,256]{1,0:T(8,128)}) custom-call(bf16[256,256]{1,0:T(8,128)(2,1)} %get-tuple-element.6.a_ref, f32[256,256]{1,0:T(8,128)} %get-tuple-element.7.b_ref, f32[256,256]{1,0:T(8,128)} %get-tuple-element.8.c_ref), custom_call_target="tpu_custom_call" | custom-call | bytes 1310720 | tf_op jit(solution)/shard_map/pallas_call | solution.py:452
  (8 shorter events, 0.1 us)
where the time goes:
time: 73.1 us; the launch traced here: 72.9 us
  Pallas kernels  70 us (96%)
  other arithmetic  1.42 us (2%)
  local copies, waits for them, and re-layouts  0.74 us (1%)
    pallas_call x1, Pallas kernels, on_device(): pl.pallas_call(functools.partial(layer_kernel, (rows, reps, quart, slots,...  49 us
    pallas_call x1, Pallas kernels, on_device(): pl.pallas_call(store_kernel, out_shape=tuple((jax.ShapeDtypeStruct(r.shap...  21 us

commit v1 on v0

--- a/solution.py
+++ b/solution.py
@@ -94,17 +94,81 @@
     def section(ref, j):
         return ref.at[pl.ds(j * quart, quart)]
 
-    def feature_copy(d):
-        return remote(
-            own, section(window, HALF - d), a_send.at[HALF - d], a_recv.at[HALF - d],
-            (row + d, rep),
-        )
-
+    side = 1 - 2 * (row % 2)
+    odd = row % 2
+    peer = row + side
+    first = quart // 2
+
+    def piece(off, part):
+        start, size = ((0, quart), (0, first), (first, quart - first))[part]
+        return window.at[pl.ds((HALF + off) * quart + start, size)]
+
+    def feature_copy(k):
+        src, dst, target = (
+            (own, piece(-side, 0), peer),
+            (own, piece(-2, 0), row + 2),
+            (own, piece(2, 0), row - 2),
+            (piece(side, 1), piece(side - 2, 1), row + 2),
+            (piece(side, 1), piece(side + 2, 1), row - 2),
+            (piece(2, 2), piece(2 - side, 2), peer),
+            (piece(-2, 2), piece(-2 - side, 2), peer),
+            (piece(-side, 0), piece(-3 * side, 0), row + 2 * side),
+        )[k]
+        return remote(src, dst, a_send.at[k], a_recv.at[k], (target, rep))
+
+    def feature_wait(sem, part):
+        spot = piece(0, part)
+        remote(spot, spot, a_send.at[0], a_recv.at[sem], (peer, rep)).wait_recv()
+
+    above, below = inside(2), inside(-2)
+    sends = (
+        None, above, below, above, below, above, below,
+        jnp.logical_and(inside(-side), inside(2 * side)),
+    )
+
+    def start_feature(k):
+        if sends[k] is None:
+            feature_copy(k).start()
+        else:
+            @pl.when(sends[k])
+            def _():
+                feature_copy(k).start()
+
+    for k in (0, 1, 2):
+        start_feature(k)
+    vals_copy.wait()
+
+    turned[pairs] = jnp.zeros((blk, blk), turned.dtype)
+
+    def turn(p, carry):
+        turned[p] = vals[p].T
+        return carry
+
+    lax.fori_loop(0, pairs // 2, turn, 0, unroll=8)
+    feature_wait(0, 0)
+    start_feature(3)
+    start_feature(4)
+
+    @pl.when(above)
+    def _():
+        feature_wait(2, 0)
+
+    start_feature(5)
+
+    @pl.when(below)
+    def _():
+        feature_wait(1, 0)
+
+    start_feature(6)
+    lax.fori_loop(pairs // 2, pairs, turn, 0, unroll=8)
+
+    @pl.when(inside(-side))
+    def _():
+        feature_wait(3 + odd, 1)
+        feature_wait(6 - odd, 2)
+
+    start_feature(7)
     for d in offsets:
-        @pl.when(inside(d))
-        def _():
-            feature_copy(d).start()
-
         @pl.when(jnp.logical_not(inside(d)))
         def _():
             for q in range(quart):
@@ -112,25 +176,18 @@
                 back_recv[(HALF + d) * quart + q] = jnp.zeros(
                     back_recv.shape[1:], back_recv.dtype
                 )
-    vals_copy.wait()
-
-    turned[pairs] = jnp.zeros((blk, blk), turned.dtype)
-
-    def turn(p, carry):
-        turned[p] = vals[p].T
-        return carry
-
-    lax.fori_loop(0, pairs, turn, 0, unroll=8)
     own_copy.wait()
     weight_copy.wait()
     cotangent_copy.wait()
-    for d in offsets:
-        @pl.when(inside(d))
-        def _():
-            remote(
-                own, section(window, HALF + d), a_send.at[HALF + d], a_recv.at[HALF + d],
-                (row + d, rep),
-            ).wait_recv()
+
+    @pl.when(inside(3 * side))
+    def _():
+        feature_wait(4 - odd, 1)
+        feature_wait(5 + odd, 2)
+
+    @pl.when(inside(-3 * side))
+    def _():
+        feature_wait(7, 0)
 
     def partial(b):
         total = None
@@ -325,8 +382,14 @@
     for d in offsets:
         @pl.when(inside(d))
         def _():
-            feature_copy(d).wait_send()
             grad_copy(d).wait_send()
+    for k in range(len(sends)):
+        if sends[k] is None:
+            feature_copy(k).wait_send()
+        else:
+            @pl.when(sends[k])
+            def _():
+                feature_copy(k).wait_send()
     for mask in masks:
         part_copy(mask - 1).wait_send()
         back_copy(mask - 1).wait_send()
@@ -337,15 +400,21 @@
         row_copy(k).wait_send()
 
 
-def store_kernel(a_ref, b_ref, c_ref, a_out, b_out, c_out, sems):
-    copies = [
-        pltpu.make_async_copy(src, dst, sems.at[k])
-        for k, (src, dst) in enumerate(((a_ref, a_out), (b_ref, b_out), (c_ref, c_out)))
-    ]
-    for copy in copies:
-        copy.start()
-    for copy in copies:
-        copy.wait()
+def store_kernel(
+    a_ref, b_ref, c_ref, a_out, b_out, c_out, a_held, b_held, c_held, in_sems, out_sems
+):
+    ways = ((a_ref, a_held, a_out), (b_ref, b_held, b_out), (c_ref, c_held, c_out))
+    fetches, stores = [], []
+    for k, (src, held, dst) in enumerate(ways):
+        fetches.append(pltpu.make_async_copy(src, held, in_sems.at[k]))
+        stores.append(pltpu.make_async_copy(held, dst, out_sems.at[k]))
+    for fetch in fetches:
+        fetch.start()
+    for fetch, store in zip(fetches, stores):
+        fetch.wait()
+        store.start()
+    for store in stores:
+        store.wait()
 
 
 def make_plan(block_cols, quart):
@@ -396,7 +465,7 @@
     dma = pltpu.SemaphoreType.DMA
     bf16, f32 = jnp.bfloat16, jnp.float32
     vmem = pl.BlockSpec(memory_space=pltpu.VMEM)
-    hbm = pl.BlockSpec(memory_space=pl.ANY)
+    hbm = pl.BlockSpec(memory_space=pltpu.HBM)
     results = pl.pallas_call(
         functools.partial(layer_kernel, (rows, reps, quart, slots, blk, blocks)),
         out_shape=(
@@ -427,7 +496,7 @@
             pltpu.VMEM((levels, share, hidden), f32),
             pltpu.VMEM((hidden, hidden), f32),
             dma((4,)),
-            dma((SECTIONS,)), dma((SECTIONS,)),
+            dma((8,)), dma((8,)),
             dma((reps - 1,)), dma((reps - 1,)),
             dma((reps - 1,)), dma((reps - 1,)),
             dma((SECTIONS,)), dma((SECTIONS,)),
@@ -454,7 +523,7 @@
         out_shape=tuple(jax.ShapeDtypeStruct(r.shape, r.dtype) for r in results),
         in_specs=[hbm, hbm, hbm],
         out_specs=(hbm, hbm, hbm),
-        scratch_shapes=[dma((3,))],
+        scratch_shapes=[pltpu.VMEM(r.shape, r.dtype) for r in results] + [dma((3,)), dma((3,))],
         compiler_params=pltpu.CompilerParams(vmem_limit_bytes=60 * 1024 * 1024),
         cost_estimate=pl.CostEstimate(
             flops=0, bytes_accessed=20 * own_rows * hidden, transcendentals=0

time: 73.1 us -> 54.9 us (0.75)
  Pallas kernels: 70 us -> 51.8 us
    pallas_call x1, Pallas kernels: 21 us -> 1.86 us  [on_device(): pl.pallas_call(store_kernel, out_shape=tuple((jax.ShapeDtypeStruct(r.shap...]
    pallas_call x1, Pallas kernels: 49 us -> 50 us  [on_device(): pl.pallas_call(functools.partial(layer_kernel, (rows, reps, quart, slots,...]
where the time goes in v1:
time: 54.9 us; the launch traced here: 54.7 us
  Pallas kernels  51.8 us (94%)
  other arithmetic  1.42 us (3%)
  local copies, waits for them, and re-layouts  0.74 us (1%)
  between operations  0.7 us (1%)
    pallas_call x1, Pallas kernels, on_device(): pl.pallas_call(functools.partial(layer_kernel, (rows, reps, quart, slots,...  50 us
    pallas_call x1, Pallas kernels, on_device(): pl.pallas_call(store_kernel, out_shape=tuple((jax.ShapeDtypeStruct(r.shap...  1.86 us

profile of v1, /device:TPU:10, one launch (start us, length us, event | category | flops | bytes accessed | tf_op | source)
XLA Modules:
  0.0 54.7 jit_solution(12451188218970167202)
XLA Ops:
  0.7 0.7 %subtract_reduce_fusion = s32[8,12]{1,0:T(8,128)S(1)} fusion(s32[8,1,12]{2,1,0:T(1,128)} %param.6, s32[]{:T(128)S(6)} %add.158), kind=kLoop, calls=%fused_computation.16 | loop fusion | flops 96 | bytes 772 | tf_op jit(solution)/shard_map/sub | solution.py:425
  1.4 0.1 sub.77
  1.5 0.1 convert_reduce_fusion.2
  1.6 0.1 convert_reduce_fusion
  1.7 0.1 select_reduce_fusion.3
  1.8 0.1 convert_reduce_fusion.1
  1.9 0.1 select_reduce_fusion.2
  2.0 0.1 select_reduce_fusion
  2.2 0.7 %concatenate.3.plan_ref = s32[462]{0:T(512)} concatenate(s32[96]{0:T(128)S(1)} %get-tuple-element.12, s32[124]{0:T(128)S(1)} %broadcast_add_fusion, s32[124]{0:T(128)S(1)} %get-tuple-element.9, s32[62]{0:T(128)S(1)} %broadcast_subtract_fusion, s32[28]{0:T(128)S(1)} %get-tuple-element.13, s32[28]{0:T(128)S(1)} %convert_reduce_fusion.2), dimensions={0} | concatenate | bytes 3696 | tf_op jit(solution)/shard_map/concatenate | solution.py:452
  2.8 50.0 %shard_map.76 = (bf16[256,256]{1,0:T(8,128)(2,1)}, f32[256,256]{1,0:T(8,128)}, f32[256,256]{1,0:T(8,128)}) custom-call(s32[462]{0:T(512)} %concatenate.3.plan_ref, bf16[8,128,256]{2,1,0:T(8,128)(2,1)} %bitcast.3, bf16[96,128,128]{2,1,0:T(8,128)(2,1)} %bitcast.2, bf16[256,256]{1,0:T(8,128)(2,1)} %weight_ref.1, bf16[256,256]{1,0:T(8,128)(2,1)} %cotangent_ref.1), custom_call_target="tpu_custom_call" | custom-call | flops 1610612736 | bytes 3145728 | tf_op jit(solution)/shard_map/pallas_call | solution.py:469
  52.8 1.9 %shard_map.77 = (bf16[256,256]{1,0:T(8,128)(2,1)}, f32[256,256]{1,0:T(8,128)}, f32[256,256]{1,0:T(8,128)}) custom-call(bf16[256,256]{1,0:T(8,128)(2,1)} %get-tuple-element.6.a_ref, f32[256,256]{1,0:T(8,128)} %get-tuple-element.7.b_ref, f32[256,256]{1,0:T(8,128)} %get-tuple-element.8.c_ref), custom_call_target="tpu_custom_call" | custom-call | bytes 1310720 | tf_op jit(solution)/shard_map/pallas_call | solution.py:521
  (8 shorter events, 0.1 us)

commit v2 on v1

--- a/solution.py
+++ b/solution.py
@@ -40,7 +40,7 @@
     plan_ref, features_ref, vals_ref, weight_ref, cotangent_ref,
     out_ref, grad_weight_ref, grad_features_ref,
     vals, turned, weight_own, cotangent, window, part_send, part_recv, near, far, run,
-    back_send, back_recv, gw_send, gw_recv, gw_half, gw_across, bf_send, bf_recv, gw_all,
+    back_send, back_recv, long_recv, gw_send, gw_recv, gw_half, gw_across, bf_send, bf_recv, gw_all,
     local_sem, a_send, a_recv, b_send, b_recv, c_send, c_recv,
     d_send, d_recv, e_send, e_recv, f_send, f_recv, g_send, g_recv,
 ):
@@ -285,9 +285,6 @@
         )
 
     beside_copy().start()
-    beside_copy().wait_recv()
-    gw_half[...] = gw_send[pl.ds(core * half_rows, half_rows)] + gw_recv[...]
-    across_copy().start()
     back_copy(1).wait_recv()
 
     def backward(source, start, stop, acc):
@@ -314,12 +311,16 @@
     half = steps // 2
     fifth = half // 10 * 5
     acc = backward(near, 0, fifth, zeros)
+    beside_copy().wait_recv()
+    gw_half[...] = gw_send[pl.ds(core * half_rows, half_rows)] + gw_recv[...]
+    across_copy().start()
     back_copy(0).wait_recv()
     back_copy(2).start()
+    acc = backward(near, fifth, fifth + 10, acc)
     across_copy().wait_recv()
     bf_send[0] = gw_half[pl.ds(chip * share, share)] + gw_across[...]
     row_copy(0).start()
-    backward(near, fifth, half, acc)
+    backward(near, fifth + 10, half, acc)
     back_copy(2).wait_recv()
     row_copy(0).wait_recv()
     bf_send[1] = bf_send[0] + bf_recv[0]
@@ -338,19 +339,51 @@
             found.append(jnp.where(some > 0, run[last], 0.0))
         return found[0] + found[1]
 
-    def grad_copy(d):
-        return remote(
-            section(back_send, HALF + d), section(back_recv, HALF - d), d_send.at[HALF - d],
-            d_recv.at[HALF - d], (row + d, rep),
-        )
-
-    for d in offsets:
+    def grad_copy(off):
+        return remote(
+            section(back_send, HALF + off), section(back_recv, HALF - off),
+            d_send.at[HALF + off], d_recv.at[HALF - off], (row + off, rep),
+        )
+
+    def long_copy():
+        return remote(
+            section(back_send, HALF - 3 * side), long_recv, d_send.at[HALF - 3 * side],
+            d_recv.at[HALF], (row - 2 * side, rep),
+        )
+
+    def put_section(off, added=None):
         for q in range(quart):
-            back_send[(HALF + d) * quart + q] = section_sum(HALF + d, q).astype(jnp.bfloat16)
-
-        @pl.when(inside(d))
+            value = section_sum(HALF + off, q)
+            if added is not None:
+                value = value + added[q].astype(jnp.float32)
+            back_send[(HALF + off) * quart + q] = value.astype(jnp.bfloat16)
+
+    @pl.when(inside(-3 * side))
+    def _():
+        put_section(-3 * side)
+        long_copy().start()
+
+    direct = (3 * side, 2, -2, side)
+    for off in direct:
+        @pl.when(inside(off))
         def _():
-            grad_copy(d).start()
+            put_section(off)
+            grad_copy(off).start()
+
+    has_long = jnp.logical_and(inside(2 * side), inside(-side))
+
+    @pl.when(has_long)
+    def _():
+        remote(
+            long_recv, long_recv, d_send.at[HALF], d_recv.at[HALF], (row + 2 * side, rep)
+        ).wait_recv()
+        put_section(-side, long_recv)
+        grad_copy(-side).start()
+
+    @pl.when(jnp.logical_and(inside(-side), jnp.logical_not(inside(2 * side))))
+    def _():
+        put_section(-side)
+        grad_copy(-side).start()
 
     for k in range(2, len(bits)):
         row_copy(k).wait_recv()
@@ -362,27 +395,33 @@
     for mask in masks:
         gather_copy(mask, rep).start()
 
-    for d in reversed(offsets):
-        @pl.when(inside(d))
+    sources = (side, 2, -2, 3 * side, -side)
+    for off in sources:
+        @pl.when(inside(off))
         def _():
             remote(
-                section(back_send, HALF + d), section(back_recv, HALF + d), d_send.at[HALF + d],
-                d_recv.at[HALF + d], (row + d, rep),
+                section(back_send, HALF + off), section(back_recv, HALF + off),
+                d_send.at[HALF + off], d_recv.at[HALF + off], (row + off, rep),
             ).wait_recv()
     for q in range(quart):
         result = section_sum(HALF, q)
-        for d in offsets:
-            result = result + back_recv[(HALF + d) * quart + q].astype(jnp.float32)
+        for off in sources:
+            result = result + back_recv[(HALF + off) * quart + q].astype(jnp.float32)
         grad_features_ref[q * blk:(q + 1) * blk] = result
 
     for mask in reversed(masks):
         gather_copy(mask, flip_all(rep, mask)).wait_recv()
     grad_weight_ref[...] = gw_all[...] * (rows * blocks * blk) ** (-0.5)
 
-    for d in offsets:
-        @pl.when(inside(d))
+    for off in direct + (-side,):
+        @pl.when(inside(off))
         def _():
-            grad_copy(d).wait_send()
+            grad_copy(off).wait_send()
+
+    @pl.when(inside(-3 * side))
+    def _():
+        long_copy().wait_send()
+
     for k in range(len(sends)):
         if sends[k] is None:
             feature_copy(k).wait_send()
@@ -488,6 +527,7 @@
             pltpu.VMEM((pairs // 2 + SECTIONS * quart, blk, hidden), f32),
             pltpu.VMEM((SECTIONS * quart, blk, hidden), bf16),
             pltpu.VMEM((SECTIONS * quart, blk, hidden), bf16),
+            pltpu.VMEM((quart, blk, hidden), bf16),
             pltpu.VMEM((hidden, hidden), f32),
             pltpu.VMEM((2 * share, hidden), f32),
             pltpu.VMEM((2 * share, hidden), f32),

time: 54.9 us -> 52.5 us (0.956)
  Pallas kernels: 51.8 us -> 49.4 us
    pallas_call x1, Pallas kernels: 50 us -> 47.5 us  [on_device(): pl.pallas_call(functools.partial(layer_kernel, (rows, reps, quart, slots,...]
where the time goes in v2:
time: 52.5 us; the launch traced here: 52.3 us
  Pallas kernels  49.4 us (94%)
  other arithmetic  1.42 us (3%)
  local copies, waits for them, and re-layouts  0.74 us (1%)
  between operations  0.7 us (1%)
    pallas_call x1, Pallas kernels, on_device(): pl.pallas_call(functools.partial(layer_kernel, (rows, reps, quart, slots,...  47.5 us
    pallas_call x1, Pallas kernels, on_device(): pl.pallas_call(store_kernel, out_shape=tuple((jax.ShapeDtypeStruct(r.shap...  1.86 us

profile of v2, /device:TPU:10, one launch (start us, length us, event | category | flops | bytes accessed | tf_op | source)
XLA Modules:
  0.0 52.3 jit_solution(15449702685070714281)
XLA Ops:
  0.7 0.7 %subtract_reduce_fusion = s32[8,12]{1,0:T(8,128)S(1)} fusion(s32[8,1,12]{2,1,0:T(1,128)} %param.6, s32[]{:T(128)S(6)} %add.158), kind=kLoop, calls=%fused_computation.16 | loop fusion | flops 96 | bytes 772 | tf_op jit(solution)/shard_map/sub | solution.py:464
  1.4 0.1 sub.77
  1.5 0.1 convert_reduce_fusion.2
  1.6 0.1 convert_reduce_fusion
  1.7 0.1 select_reduce_fusion.3
  1.8 0.1 convert_reduce_fusion.1
  1.9 0.1 select_reduce_fusion.2
  2.0 0.1 select_reduce_fusion
  2.2 0.7 %concatenate.3.plan_ref = s32[462]{0:T(512)} concatenate(s32[96]{0:T(128)S(1)} %get-tuple-element.12, s32[124]{0:T(128)S(1)} %broadcast_add_fusion, s32[124]{0:T(128)S(1)} %get-tuple-element.9, s32[62]{0:T(128)S(1)} %broadcast_subtract_fusion, s32[28]{0:T(128)S(1)} %get-tuple-element.13, s32[28]{0:T(128)S(1)} %convert_reduce_fusion.2), dimensions={0} | concatenate | bytes 3696 | tf_op jit(solution)/shard_map/concatenate | solution.py:491
  2.8 47.5 %shard_map.76 = (bf16[256,256]{1,0:T(8,128)(2,1)}, f32[256,256]{1,0:T(8,128)}, f32[256,256]{1,0:T(8,128)}) custom-call(s32[462]{0:T(512)} %concatenate.3.plan_ref, bf16[8,128,256]{2,1,0:T(8,128)(2,1)} %bitcast.3, bf16[96,128,128]{2,1,0:T(8,128)(2,1)} %bitcast.2, bf16[256,256]{1,0:T(8,128)(2,1)} %weight_ref.1, bf16[256,256]{1,0:T(8,128)(2,1)} %cotangent_ref.1), custom_call_target="tpu_custom_call" | custom-call | flops 1610612736 | bytes 3145728 | tf_op jit(solution)/shard_map/pallas_call | solution.py:508
  50.4 1.9 %shard_map.77 = (bf16[256,256]{1,0:T(8,128)(2,1)}, f32[256,256]{1,0:T(8,128)}, f32[256,256]{1,0:T(8,128)}) custom-call(bf16[256,256]{1,0:T(8,128)(2,1)} %get-tuple-element.6.a_ref, f32[256,256]{1,0:T(8,128)} %get-tuple-element.7.b_ref, f32[256,256]{1,0:T(8,128)} %get-tuple-element.8.c_ref), custom_call_target="tpu_custom_call" | custom-call | bytes 1310720 | tf_op jit(solution)/shard_map/pallas_call | solution.py:561
  (8 shorter events, 0.1 us)

commit v3 on v2

--- a/solution.py
+++ b/solution.py
@@ -37,11 +37,11 @@
 
 def layer_kernel(
     sizes,
-    plan_ref, features_ref, vals_ref, weight_ref, cotangent_ref,
+    cols_ref, features_ref, vals_ref, weight_ref, cotangent_ref,
     out_ref, grad_weight_ref, grad_features_ref,
     vals, turned, weight_own, cotangent, window, part_send, part_recv, near, far, run,
     back_send, back_recv, long_recv, gw_send, gw_recv, gw_half, gw_across, bf_send, bf_recv, gw_all,
-    local_sem, a_send, a_recv, b_send, b_recv, c_send, c_recv,
+    plan_held, plan_ref, local_sem, a_send, a_recv, b_send, b_recv, c_send, c_recv,
     d_send, d_recv, e_send, e_recv, f_send, f_recv, g_send, g_recv,
 ):
     rows, reps, quart, slots, blk, blocks = sizes
@@ -91,6 +91,13 @@
         )
     pl.semaphore_wait(barrier, expected)
 
+    base_col = (row - HALF) * blocks + rep * quart
+
+    def slot_of(b, s):
+        moved = cols_ref[b, 0, s] - base_col
+        slot = lax.div(moved, blocks) * quart + lax.rem(moved, blocks)
+        return jnp.minimum(jnp.maximum(slot, 0), spots - 1)
+
     def section(ref, j):
         return ref.at[pl.ds(j * quart, quart)]
 
@@ -136,6 +143,17 @@
 
     for k in (0, 1, 2):
         start_feature(k)
+
+    lane = lax.broadcasted_iota(jnp.int32, (1, 128), 1)
+    bins = jnp.full((1, 128), 1000, jnp.int32)
+    for b in range(blocks):
+        away = jnp.where(rep // 2 == (2 * b) // blocks, 0, spots)
+        for s in range(slots):
+            bins = jnp.where(lane == b * slots + s, slot_of(b, s) + away, bins)
+    for k, line in enumerate(make_plan(bins, pairs, slots, blocks, spots)):
+        plan_held[k:k + 1] = line
+    plan_copy = pltpu.make_async_copy(plan_held, plan_ref, local_sem.at[4])
+    plan_copy.start()
     vals_copy.wait()
 
     turned[pairs] = jnp.zeros((blk, blk), turned.dtype)
@@ -179,6 +197,7 @@
     own_copy.wait()
     weight_copy.wait()
     cotangent_copy.wait()
+    plan_copy.wait()
 
     @pl.when(inside(3 * side))
     def _():
@@ -194,7 +213,7 @@
         for s in range(0, slots, 2):
             left = jnp.concatenate([vals[b * slots + s], vals[b * slots + s + 1]], axis=1)
             right = jnp.concatenate(
-                [window[plan_ref[b * slots + s]], window[plan_ref[b * slots + s + 1]]], axis=0
+                [window[slot_of(b, s)], window[slot_of(b, s + 1)]], axis=0
             )
             term = jnp.dot(left, right, preferred_element_type=jnp.float32)
             total = term if total is None else total + term
@@ -290,16 +309,16 @@
     def backward(source, start, stop, acc):
         def step(k, acc):
             left = jnp.concatenate(
-                [turned[plan_ref[pairs + 2 * k]], turned[plan_ref[pairs + 2 * k + 1]]], axis=1
+                [turned[plan_ref[0, 2 * k]], turned[plan_ref[0, 2 * k + 1]]], axis=1
             )
             right = jnp.concatenate(
                 [
-                    source[plan_ref[pairs + padded + 2 * k]],
-                    source[plan_ref[pairs + padded + 2 * k + 1]],
+                    source[plan_ref[1, 2 * k]],
+                    source[plan_ref[1, 2 * k + 1]],
                 ],
                 axis=0,
             )
-            keep = plan_ref[pairs + 2 * padded + k]
+            keep = plan_ref[2, k]
             term = jnp.dot(left, right, preferred_element_type=jnp.float32)
             acc = jnp.where(keep > 0, acc, 0.0) + term
             run[k] = acc
@@ -334,8 +353,8 @@
     def section_sum(j, q):
         found = []
         for c in (j * quart + q, spots + j * quart + q):
-            last = plan_ref[pairs + 2 * padded + steps + c]
-            some = plan_ref[pairs + 2 * padded + steps + 2 * spots + c]
+            last = plan_ref[3, c]
+            some = plan_ref[4, c]
             found.append(jnp.where(some > 0, run[last], 0.0))
         return found[0] + found[1]
 
@@ -456,39 +475,39 @@
         store.wait()
 
 
-def make_plan(block_cols, quart):
-    blocks, slots = block_cols.shape
-    pairs = blocks * slots
-    spots = SECTIONS * quart
-    first = (lax.axis_index("row") - HALF) * blocks + lax.axis_index("rep") * quart
-    moved = block_cols.reshape(pairs) - first
-    slot = (moved // blocks) * quart + moved % blocks
-    order = jnp.arange(pairs, dtype=jnp.int32)
-    far = (order // slots // quart) // 2 != lax.axis_index("rep") // 2
-    bin_of = slot + jnp.where(far, spots, 0)
-    spot = jnp.arange(2 * spots, dtype=jnp.int32)
+def make_plan(bins, pairs, slots, blocks, spots):
+    side = bins.shape[1]
     half = (pairs // 2 + spots) // 2
-    count = jnp.sum((bin_of[:, None] == spot[None, :]).astype(jnp.int32), axis=0)
-    width = (count + 1) // 2
-    same_half = (spot[:, None] // spots) == (spot[None, :] // spots)
-    before = same_half & (spot[:, None] < spot[None, :])
-    start = jnp.sum(jnp.where(before, width[:, None], 0), axis=0) + half * (spot // spots)
-    rank = jnp.sum(
-        ((bin_of[:, None] == bin_of[None, :]) & (order[:, None] < order[None, :])).astype(
-            jnp.int32
-        ),
-        axis=0,
-    )
-    base = jnp.sum(jnp.where(spot[None, :] == bin_of[:, None], start[None, :], 0), axis=1)
-    place = 2 * base + rank
-    hot = place[:, None] == jnp.arange(4 * half, dtype=jnp.int32)[None, :]
-    pair = pairs + jnp.sum(jnp.where(hot, order[:, None] - pairs, 0), axis=0)
-    block = jnp.sum(jnp.where(hot, order[:, None] // slots % (2 * quart), 0), axis=0)
-    step = jnp.arange(2 * half, dtype=jnp.int32)
-    first_of = (start[:, None] == step[None, :]) & (count[:, None] > 0)
-    keep = 1 - jnp.sum(first_of.astype(jnp.int32), axis=0)
+    row_of = lax.broadcasted_iota(jnp.int32, (side, side), 0)
+    col_of = lax.broadcasted_iota(jnp.int32, (side, side), 1)
+    lane = lax.broadcasted_iota(jnp.int32, (1, side), 1)
+
+    def across(line):
+        return jnp.broadcast_to(line, (side, side))
+
+    def total(mask, value):
+        return jnp.sum(jnp.where(mask, value, 0), axis=0, keepdims=True)
+
+    bin_col = across(bins)
+    bin_row = bin_col.T
+    rank = total((bin_row == bin_col) & (row_of < col_of), 1)
+    count = total(bin_row == col_of, 1)
+    width = lax.shift_right_logical(count + 1, 1)
+    same = (row_of >= spots) == (col_of >= spots)
+    start = total((row_of < col_of) & same, across(width).T) + jnp.where(lane >= spots, half, 0)
+    start_row = across(jnp.where((count > 0) & (lane < 2 * spots), start, -1)).T
+    base = total(row_of == bin_col, start_row)
+    place = jnp.where(lane < pairs, 2 * base + rank, -1)
+    hot = across(place).T == col_of
+    pair = pairs + total(hot, row_of - pairs)
+    block_row = jnp.zeros((side, side), jnp.int32)
+    for b in range(1, blocks):
+        step = 1 if b != blocks // 2 else 1 - blocks // 2
+        block_row = block_row + jnp.where(row_of >= b * slots, step, 0)
+    block = total(hot, block_row)
+    keep = 1 - total(start_row == col_of, 1)
     last = jnp.maximum(start + width - 1, 0)
-    return jnp.concatenate([slot, pair, block, keep, last, count])
+    return pair, block, keep, last, count
 
 
 def on_device(rows, reps, features, block_cols, block_vals, weight, cotangent):
@@ -500,7 +519,6 @@
     own_rows = quart * blk
     levels = rows.bit_length() - 1
     share = hidden // reps
-    plan = make_plan(block_cols[:, 0, :], quart)
     dma = pltpu.SemaphoreType.DMA
     bf16, f32 = jnp.bfloat16, jnp.float32
     vmem = pl.BlockSpec(memory_space=pltpu.VMEM)
@@ -535,7 +553,9 @@
             pltpu.VMEM((levels, share, hidden), f32),
             pltpu.VMEM((levels, share, hidden), f32),
             pltpu.VMEM((hidden, hidden), f32),
-            dma((4,)),
+            pltpu.VMEM((8, 128), jnp.int32),
+            pltpu.SMEM((8, 128), jnp.int32),
+            dma((5,)),
             dma((8,)), dma((8,)),
             dma((reps - 1,)), dma((reps - 1,)),
             dma((reps - 1,)), dma((reps - 1,)),
@@ -552,7 +572,7 @@
             transcendentals=own_rows * hidden,
         ),
     )(
-        plan,
+        block_cols,
         features.reshape(blocks, blk, hidden),
         block_vals.reshape(pairs, blk, blk),
         weight,

time: 52.5 us -> 50.3 us (0.958)
  other arithmetic: 1.42 us -> 0 us
  local copies, waits for them, and re-layouts: 0.74 us -> 0 us
    sub x2 -> x0, other arithmetic: 0.71 us -> none  [the longest x1 0.7 us: make_plan(): moved = block_cols.reshape(pairs) - first]
    concatenate x1 -> x0, local copies, waits for them, and re-layouts: 0.67 us -> none  [make_plan(): return jnp.concatenate([slot, pair, block, keep, last, count])]
    reduce_sum x6 -> x0, other arithmetic: 0.61 us -> none  [the longest x1 0.12 us: make_plan(): jnp.sum(jnp.where(hot, order[:, None] // slots % (2 * quart), 0), axis=0)]
where the time goes in v3:
time: 50.3 us; the launch traced here: 50.1 us
  Pallas kernels  49.5 us (98%)
  between operations  0.64 us (1%)
    pallas_call x1, Pallas kernels, on_device(): pl.pallas_call(functools.partial(layer_kernel, (rows, reps, quart, slots,...  47.6 us
    pallas_call x1, Pallas kernels, on_device(): pl.pallas_call(store_kernel, out_shape=tuple((jax.ShapeDtypeStruct(r.shap...  1.86 us

profile of v3, /device:TPU:10, one launch (start us, length us, event | category | flops | bytes accessed | tf_op | source)
XLA Modules:
  0.0 50.1 jit_solution(4514334118632034456)
XLA Ops:
  0.6 47.6 %shard_map.76 = (bf16[256,256]{1,0:T(8,128)(2,1)}, f32[256,256]{1,0:T(8,128)}, f32[256,256]{1,0:T(8,128)}) custom-call(s32[8,1,12]{2,1,0:T(1,128)} %cols_ref.1, bf16[8,128,256]{2,1,0:T(8,128)(2,1)} %bitcast.3, bf16[96,128,128]{2,1,0:T(8,128)(2,1)} %bitcast.2, bf16[256,256]{1,0:T(8,128)(2,1)} %weight_ref.1, bf16[256,256]{1,0:T(8,128)(2,1)} %cotangent_ref.1), custom_call_target="tpu_custom_call" | custom-call | flops 1610612736 | bytes 3145728 | tf_op jit(solution)/shard_map/pallas_call | solution.py:526
  48.3 1.9 %shard_map.77 = (bf16[256,256]{1,0:T(8,128)(2,1)}, f32[256,256]{1,0:T(8,128)}, f32[256,256]{1,0:T(8,128)}) custom-call(bf16[256,256]{1,0:T(8,128)(2,1)} %get-tuple-element.6.a_ref, f32[256,256]{1,0:T(8,128)} %get-tuple-element.7.b_ref, f32[256,256]{1,0:T(8,128)} %get-tuple-element.8.c_ref), custom_call_target="tpu_custom_call" | custom-call | bytes 1310720 | tf_op jit(solution)/shard_map/pallas_call | solution.py:581

commit v4 on v3

--- a/solution.py
+++ b/solution.py
@@ -178,7 +178,6 @@
         feature_wait(1, 0)
 
     start_feature(6)
-    lax.fori_loop(pairs // 2, pairs, turn, 0, unroll=8)
 
     @pl.when(inside(-side))
     def _():
@@ -186,6 +185,7 @@
         feature_wait(6 - odd, 2)
 
     start_feature(7)
+    lax.fori_loop(pairs // 2, pairs, turn, 0, unroll=8)
     for d in offsets:
         @pl.when(jnp.logical_not(inside(d)))
         def _():

time: 50.3 us -> 50.3 us (level)
  no operation moved by 1% of the time
where the time goes in v4:
time: 50.3 us; the launch traced here: 50.1 us
  Pallas kernels  49.5 us (98%)
  between operations  0.64 us (1%)
    pallas_call x1, Pallas kernels, on_device(): pl.pallas_call(functools.partial(layer_kernel, (rows, reps, quart, slots,...  47.6 us
    pallas_call x1, Pallas kernels, on_device(): pl.pallas_call(store_kernel, out_shape=tuple((jax.ShapeDtypeStruct(r.shap...  1.86 us

profile of v4, /device:TPU:10, one launch (start us, length us, event | category | flops | bytes accessed | tf_op | source)
XLA Modules:
  0.0 50.1 jit_solution(5716334012650669407)
XLA Ops:
  0.6 47.6 %shard_map.76 = (bf16[256,256]{1,0:T(8,128)(2,1)}, f32[256,256]{1,0:T(8,128)}, f32[256,256]{1,0:T(8,128)}) custom-call(s32[8,1,12]{2,1,0:T(1,128)} %cols_ref.1, bf16[8,128,256]{2,1,0:T(8,128)(2,1)} %bitcast.3, bf16[96,128,128]{2,1,0:T(8,128)(2,1)} %bitcast.2, bf16[256,256]{1,0:T(8,128)(2,1)} %weight_ref.1, bf16[256,256]{1,0:T(8,128)(2,1)} %cotangent_ref.1), custom_call_target="tpu_custom_call" | custom-call | flops 1610612736 | bytes 3145728 | tf_op jit(solution)/shard_map/pallas_call | solution.py:526
  48.3 1.9 %shard_map.77 = (bf16[256,256]{1,0:T(8,128)(2,1)}, f32[256,256]{1,0:T(8,128)}, f32[256,256]{1,0:T(8,128)}) custom-call(bf16[256,256]{1,0:T(8,128)(2,1)} %get-tuple-element.6.a_ref, f32[256,256]{1,0:T(8,128)} %get-tuple-element.7.b_ref, f32[256,256]{1,0:T(8,128)} %get-tuple-element.8.c_ref), custom_call_target="tpu_custom_call" | custom-call | bytes 1310720 | tf_op jit(solution)/shard_map/pallas_call | solution.py:581
